TPU v7x, 128 devices: a whole 4x4x4 slice. The times are simulated.
128 devices in a mesh: wall: 4 (over y), span: 32 (over x, z, core).
Axes of the slice: x: 4, y: 4, z: 4, core: 2. Of those that a mesh axis runs over, the one named last changes fastest.
Arguments:
- jac_lower: bfloat16 [8, 112, 112, 4096], P('wall', None, None, 'span')
- jac_inv_diag: bfloat16 [8, 112, 112, 4096], P('wall', None, None, 'span')
- jac_upper: bfloat16 [8, 112, 112, 4096], P('wall', None, None, 'span')
- residual: float32 [8, 112, 4096], P('wall', None, 'span'), may hold values from -6 to 6
- prev_update: float32 [8, 112, 4096], P('wall', None, 'span'), may hold values from -6 to 6
- send_lines: int32 [32, 32, 64], P('span'), may hold values from 0 to 127
- send_count: int32 [32, 32], P('span'), may hold values from 1 to 64, as said below
- recv_lines: int32 [32, 32, 64], P('span'), may hold values from 0 to 127
- active_lines: int32 [32], P('span'), may hold values from 64 to 128, as said below
Outputs:
- line_update: float32 [8, 112, 4096], P('wall', None, 'span')
Inputs may be any that keep to these rules, and one draw needn't show every extreme that they name: `send_count`: every sender fills all 64 slots towards at least one receiver, and one receiver gets full slots from every sender. `active_lines`: at least one device has all 128 lines live.
All inputs are finite; a program needn't handle non-finite values.
Results may differ from a plain program's by a relative error of at most 0.0003.
Values sent between devices are 32-bit elements; how exact they have to be, the bound alone decides.
A program may use at most 256 MiB of HBM per device.

v0:
```python
import jax
import jax.numpy as jnp
from jax import lax
from jax.sharding import PartitionSpec as P


def from_behind(value, axis, steps):
    count = lax.axis_size(axis)
    first, last = (max(0, -steps), min(count, count - steps))
    return lax.ppermute(value, axis, [(source, source + steps) for source in range(first, last)])


def matvec(block, vec):
    return jnp.einsum("abl,bl->al", block.astype(jnp.float32), vec, precision=lax.Precision.HIGHEST)


def lower_sweep(jac_lower, rhs, start_vec):

    def lower_step(carry, inputs):
        block, right = inputs
        value = right - matvec(block, carry)
        return (value, value)

    return lax.scan(lower_step, start_vec, (jac_lower, rhs))


def upper_sweep(jac_inv_diag, jac_upper, values, start_vec):

    def upper_step(carry, inputs):
        inverse, block, right = inputs
        value = matvec(inverse, right - matvec(block, carry))
        return (value, value)

    return lax.scan(upper_step, start_vec, (jac_inv_diag, jac_upper, values), reverse=True)


def local(
    jac_lower,
    jac_inv_diag,
    jac_upper,
    residual,
    prev_update,
    send_lines,
    send_count,
    recv_lines,
    active_lines,
):
    cells, width, _, lanes = jac_lower.shape
    spans = lax.axis_size("span")
    slot_count = send_lines.shape[2]
    lane_ids = jnp.arange(lanes, dtype=jnp.int32)
    slot_ids = jnp.arange(slot_count, dtype=jnp.int32)
    tiles = prev_update.reshape(cells * width, lanes)
    keep = (slot_ids[None, :] < send_count[0][:, None]) & (send_lines[0] < active_lines[0])
    picks = (lane_ids[:, None] == send_lines[0].reshape(-1)[None, :]) & keep.reshape(-1)[None, :]
    outgoing = jnp.dot(tiles, picks.astype(jnp.float32), precision=lax.Precision.HIGHEST)
    outgoing = outgoing.reshape(cells * width, spans, slot_count)
    incoming = lax.all_to_all(outgoing, "span", split_axis=1, concat_axis=1, tiled=True)
    landing = (recv_lines[0].reshape(-1)[:, None] == lane_ids[None, :]).astype(jnp.float32)
    coupling = jnp.dot(
        incoming.reshape(cells * width, spans * slot_count),
        landing,
        precision=lax.Precision.HIGHEST,
    )
    live = (lane_ids < active_lines[0]).astype(jnp.float32)
    rhs = (residual - coupling.reshape(cells, width, lanes)) * live[None, None, :]
    zero_vec = jnp.zeros((width, lanes), jnp.float32)
    entering = zero_vec
    for turn in range(lax.axis_size("wall") - 1):
        last, values = lower_sweep(jac_lower, rhs, entering)
        entering = from_behind(last, "wall", 1)
    last, values = lower_sweep(jac_lower, rhs, entering)
    leaving = zero_vec
    for turn in range(lax.axis_size("wall") - 1):
        first, result = upper_sweep(jac_inv_diag, jac_upper, values, leaving)
        leaving = from_behind(first, "wall", -1)
    first, result = upper_sweep(jac_inv_diag, jac_upper, values, leaving)
    return result


def solution(mesh):
    return jax.shard_map(
        local,
        mesh=mesh,
        in_specs=(
            P("wall", None, None, "span"),
            P("wall", None, None, "span"),
            P("wall", None, None, "span"),
            P("wall", None, "span"),
            P("wall", None, "span"),
            P("span", None, None),
            P("span", None),
            P("span", None, None),
            P("span"),
        ),
        out_specs=P("wall", None, "span"),
        check_vma=False,
    )
```

profile of v0, /device:TPU:0, one launch (start us, length us, event | category | flops | bytes accessed | tf_op | source)
XLA Modules:
  0.0 157.6 jit_solution(12267908807093458648)
XLA Ops:
  0.0 0.8 eq.31
  1.5 0.7 iota_compare_fusion.2
  2.2 0.1 lt.86
  2.3 0.9 convolution_bitcast_fusion
  3.2 1.8 %copy.11 = f32[224,2048]{0,1:T(8,128)} copy(f32[224,2048]{1,0:T(8,128)S(1)} %convolution_bitcast_fusion) | data formatting | bytes 3670016 | tf_op jit(solution)/shard_map/dot_general | solution.py:56
  5.1 8.4 %all-to-all-start = ((f32[224,32,64]{0,2,1:T(8,128)}), f32[224,32,64]{0,2,1:T(8,128)}, u32[]{:S(2)}, u32[]{:S(2)}) async-start(f32[224,32,64]{0,2,1:T(8,128)} %bitcast.70), calls=%async_computation | async-start | bytes 4194304 | tf_op jit(solution)/shard_map/all_to_all | solution.py:58
  13.5 28.8 %all-to-all-done = f32[224,32,64]{0,2,1:T(8,128)} async-done(((f32[224,32,64]{0,2,1:T(8,128)}), f32[224,32,64]{0,2,1:T(8,128)}, u32[]{:S(2)}, u32[]{:S(2)}) %all-to-all-start) | async-done | bytes 1835040 | tf_op jit(solution)/shard_map/all_to_all | solution.py:58
  42.3 2.6 %dot_general.72 = f32[2,112,2048]{1,0,2:T(2,128)S(1)} reshape(f32[224,32,64]{0,2,1:T(8,128)} %all-to-all-done) | data formatting | bytes 3670016 | tf_op jit(solution)/shard_map/dot_general | solution.py:60
  45.0 2.1 %fusion.9 = f32[2,112,128]{2,1,0:T(8,128)S(1)} fusion(f32[2,112,128]{2,1,0:T(8,128)S(1)} %copy-done.2, f32[2,112,2048]{1,0,2:T(2,128)S(1)} %dot_general.72, s32[2048]{0:T(1024)S(1)} %eq.34, f32[128]{0:T(128)S(1)} %compare_convert_fusion), kind=kOutput, calls=%fused_computation.31 | convolution fusion | flops 704962560 | bytes 2073088 | tf_op jit(solution)/shard_map/dot_general | solution.py:60
  47.1 6.1 %while.108 = (s32[]{:T(128)}, f32[112,128]{1,0:T(8,128)S(1)}, f32[2,112,128]{2,1,0:T(8,128)S(1)}, bf16[2,112,112,128]{3,2,1,0:T(8,128)(2,1)}, s32[]{:T(128)}, /*index=5*/s32[]{:T(128)}) while((s32[]{:T(128)}, f32[112,128]{1,0:T(8,128)S(1)}, f32[2,112,128]{2,1,0:T(8,128)S(1)}, bf16[2,112,112,128]{3,2,1,0:T(8,128)(2,1)}, s32[]{:T(128)}, ...), condition=%wide.region_1.2_spmd.clone, body=%wide.region_0.1_spmd.clone.sunk | while | flops 4831235 | bytes 3612759 | solution.py:24
  47.1 3.0 %multiply_reduce_fusion.35 = f32[128,112]{0,1:T(8,128)S(1)} fusion(f32[128,112]{0,1:T(8,128)S(1)} %select_bitcast_fusion.2, bf16[2,112,112,128]{3,2,1,0:T(8,128)(2,1)} %get-tuple-element.885, s32[]{:T(128)} %get-tuple-element.876), kind=kLoop, calls=%fused_computation.24.clone.1 | loop fusion | flops 4802560 | bytes 3325956 | tf_op jit(solution)/shard_map/while/body/eval_jaxpr/abl,bl->al/dot_general | solution.py:14
  50.2 3.0 %multiply_reduce_fusion.35 = f32[128,112]{0,1:T(8,128)S(1)} fusion(f32[128,112]{0,1:T(8,128)S(1)} %select_bitcast_fusion.2, bf16[2,112,112,128]{3,2,1,0:T(8,128)(2,1)} %get-tuple-element.885, s32[]{:T(128)} %get-tuple-element.876), kind=kLoop, calls=%fused_computation.24.clone.1 | loop fusion | flops 4802560 | bytes 3325956 | tf_op jit(solution)/shard_map/while/body/eval_jaxpr/abl,bl->al/dot_general | solution.py:14
  53.2 3.5 %collective-permute-start = (f32[112,128]{1,0:T(8,128)S(1)}, f32[112,128]{1,0:T(8,128)S(1)}, u32[]{:S(2)}, u32[]{:S(2)}) collective-permute-start(f32[112,128]{1,0:T(8,128)S(1)} %get-tuple-element.529), channel_id=1, source_target_pairs={{0,32},{32,64},{64,96},{1,33},{33,65},{65,97},{2,34},{34,66},{66,9... | collective-permute-start | bytes 172040 | tf_op jit(solution)/shard_map/ppermute | solution.py:10
  56.7 1.8 %collective-permute-done = f32[112,128]{1,0:T(8,128)S(1)} collective-permute-done((f32[112,128]{1,0:T(8,128)S(1)}, f32[112,128]{1,0:T(8,128)S(1)}, u32[]{:S(2)}, u32[]{:S(2)}) %collective-permute-start) | collective-permute-done | bytes 57376 | tf_op jit(solution)/shard_map/ppermute | solution.py:10
  58.5 6.0 %while.101 = (s32[]{:T(128)}, f32[112,128]{1,0:T(8,128)S(1)}, f32[2,112,128]{2,1,0:T(8,128)S(1)}, bf16[2,112,112,128]{3,2,1,0:T(8,128)(2,1)}, s32[]{:T(128)}) while((s32[]{:T(128)}, f32[112,128]{1,0:T(8,128)S(1)}, f32[2,112,128]{2,1,0:T(8,128)S(1)}, bf16[2,112,112,128]{3,2,1,0:T(8,128)(2,1)}, s32[]{:T(128)}) %tuple.213), condition=%wide.region_3.4_spmd, body=%wide.region_2.3_spmd.sunk | while | flops 4816898 | bytes 3498053 | solution.py:24
  58.5 3.0 %multiply_reduce_fusion.24 = f32[128,112]{0,1:T(8,128)S(1)} fusion(f32[128,112]{0,1:T(8,128)S(1)} %bitcast.228, bf16[2,112,112,128]{3,2,1,0:T(8,128)(2,1)} %get-tuple-element.901, s32[]{:T(128)} %get-tuple-element.893), kind=kLoop, calls=%fused_computation.clone.1 | loop fusion | flops 4802560 | bytes 3325956 | tf_op jit(solution)/shard_map/while/body/eval_jaxpr/abl,bl->al/dot_general | solution.py:14
  61.5 3.0 %multiply_reduce_fusion.24 = f32[128,112]{0,1:T(8,128)S(1)} fusion(f32[128,112]{0,1:T(8,128)S(1)} %bitcast.228, bf16[2,112,112,128]{3,2,1,0:T(8,128)(2,1)} %get-tuple-element.901, s32[]{:T(128)} %get-tuple-element.893), kind=kLoop, calls=%fused_computation.clone.1 | loop fusion | flops 4802560 | bytes 3325956 | tf_op jit(solution)/shard_map/while/body/eval_jaxpr/abl,bl->al/dot_general | solution.py:14
  64.5 4.3 %collective-permute-start.1 = (f32[112,128]{1,0:T(8,128)S(1)}, f32[112,128]{1,0:T(8,128)S(1)}, u32[]{:S(2)}, u32[]{:S(2)}) collective-permute-start(f32[112,128]{1,0:T(8,128)S(1)} %get-tuple-element.530), channel_id=1, source_target_pairs={{0,32},{32,64},{64,96},{1,33},{33,65},{65,97},{2,34},{34,66},{66,9... | collective-permute-start | bytes 172040 | tf_op jit(solution)/shard_map/ppermute | solution.py:10
  68.8 1.8 %collective-permute-done.1 = f32[112,128]{1,0:T(8,128)S(1)} collective-permute-done((f32[112,128]{1,0:T(8,128)S(1)}, f32[112,128]{1,0:T(8,128)S(1)}, u32[]{:S(2)}, u32[]{:S(2)}) %collective-permute-start.1) | collective-permute-done | bytes 57376 | tf_op jit(solution)/shard_map/ppermute | solution.py:10
  70.6 6.0 %while.102 = (s32[]{:T(128)}, f32[112,128]{1,0:T(8,128)S(1)}, f32[2,112,128]{2,1,0:T(8,128)S(1)}, bf16[2,112,112,128]{3,2,1,0:T(8,128)(2,1)}, s32[]{:T(128)}) while((s32[]{:T(128)}, f32[112,128]{1,0:T(8,128)S(1)}, f32[2,112,128]{2,1,0:T(8,128)S(1)}, bf16[2,112,112,128]{3,2,1,0:T(8,128)(2,1)}, s32[]{:T(128)}) %tuple.214), condition=%wide.region_5.6_spmd, body=%wide.region_4.5_spmd.sunk | while | flops 4816898 | bytes 3498053 | solution.py:24
  70.6 3.0 %multiply_reduce_fusion.25 = f32[128,112]{0,1:T(8,128)S(1)} fusion(f32[128,112]{0,1:T(8,128)S(1)} %bitcast.229, bf16[2,112,112,128]{3,2,1,0:T(8,128)(2,1)} %get-tuple-element.916, s32[]{:T(128)} %get-tuple-element.908), kind=kLoop, calls=%fused_computation.2.clone.1 | loop fusion | flops 4802560 | bytes 3325956 | tf_op jit(solution)/shard_map/while/body/eval_jaxpr/abl,bl->al/dot_general | solution.py:14
  73.6 3.0 %multiply_reduce_fusion.25 = f32[128,112]{0,1:T(8,128)S(1)} fusion(f32[128,112]{0,1:T(8,128)S(1)} %bitcast.229, bf16[2,112,112,128]{3,2,1,0:T(8,128)(2,1)} %get-tuple-element.916, s32[]{:T(128)} %get-tuple-element.908), kind=kLoop, calls=%fused_computation.2.clone.1 | loop fusion | flops 4802560 | bytes 3325956 | tf_op jit(solution)/shard_map/while/body/eval_jaxpr/abl,bl->al/dot_general | solution.py:14
  76.6 4.3 %collective-permute-start.2 = (f32[112,128]{1,0:T(8,128)S(1)}, f32[112,128]{1,0:T(8,128)S(1)}, u32[]{:S(2)}, u32[]{:S(2)}) collective-permute-start(f32[112,128]{1,0:T(8,128)S(1)} %get-tuple-element.531), channel_id=1, source_target_pairs={{0,32},{32,64},{64,96},{1,33},{33,65},{65,97},{2,34},{34,66},{66,9... | collective-permute-start | bytes 172040 | tf_op jit(solution)/shard_map/ppermute | solution.py:10
  80.9 1.8 %collective-permute-done.2 = f32[112,128]{1,0:T(8,128)S(1)} collective-permute-done((f32[112,128]{1,0:T(8,128)S(1)}, f32[112,128]{1,0:T(8,128)S(1)}, u32[]{:S(2)}, u32[]{:S(2)}) %collective-permute-start.2) | collective-permute-done | bytes 57376 | tf_op jit(solution)/shard_map/ppermute | solution.py:10
  82.7 6.1 %while.103 = (s32[]{:T(128)}, f32[112,128]{1,0:T(8,128)S(1)}, f32[2,112,128]{2,1,0:T(8,128)S(1)}, f32[2,112,128]{2,1,0:T(8,128)S(1)}, bf16[2,112,112,128]{3,2,1,0:T(8,128)(2,1)}, /*index=5*/s32[]{:T(128)}) while((s32[]{:T(128)}, f32[112,128]{1,0:T(8,128)S(1)}, f32[2,112,128]{2,1,0:T(8,128)S(1)}, f32[2,112,128]{2,1,0:T(8,128)S(1)}, ...), condition=%wide.region_7.8_spmd, body=%wide.region_6.7_spmd.sunk | while | flops 4816898 | bytes 3555405 | solution.py:24
  82.7 3.0 %multiply_reduce_fusion.26 = f32[128,112]{0,1:T(8,128)S(1)} fusion(f32[128,112]{0,1:T(8,128)S(1)} %bitcast.227, bf16[2,112,112,128]{3,2,1,0:T(8,128)(2,1)} %get-tuple-element.934, s32[]{:T(128)} %get-tuple-element.924), kind=kLoop, calls=%fused_computation.4.clone.1 | loop fusion | flops 4802560 | bytes 3325956 | tf_op jit(solution)/shard_map/while/body/eval_jaxpr/abl,bl->al/dot_general | solution.py:14
  85.8 3.0 %multiply_reduce_fusion.26 = f32[128,112]{0,1:T(8,128)S(1)} fusion(f32[128,112]{0,1:T(8,128)S(1)} %bitcast.227, bf16[2,112,112,128]{3,2,1,0:T(8,128)(2,1)} %get-tuple-element.934, s32[]{:T(128)} %get-tuple-element.924), kind=kLoop, calls=%fused_computation.4.clone.1 | loop fusion | flops 4802560 | bytes 3325956 | tf_op jit(solution)/shard_map/while/body/eval_jaxpr/abl,bl->al/dot_general | solution.py:14
  88.8 12.4 %while.104 = (s32[]{:T(128)}, f32[112,128]{0,1:T(8,128)S(1)}, f32[2,112,128]{2,1,0:T(8,128)S(1)}, bf16[2,112,112,128]{3,2,1,0:T(8,128)(2,1)}, bf16[2,112,112,128]{3,2,1,0:T(8,128)(2,1)}, /*index=5*/s32[]{:T(128)}) while((s32[]{:T(128)}, f32[112,128]{0,1:T(8,128)S(1)}, f32[2,112,128]{2,1,0:T(8,128)S(1)}, bf16[2,112,112,128]{3,2,1,0:T(8,128)(2,1)}, ...), condition=%wide.region_9.10_spmd, body=%wide.region_8.9_spmd.sunk | while | flops 9619459 | bytes 7053405 | solution.py:34
  88.8 0.1 copy.119
  88.9 3.0 %multiply_reduce_fusion.27 = f32[128,112]{0,1:T(8,128)S(1)} fusion(f32[128,112]{0,1:T(8,128)S(1)} %copy.119, bf16[2,112,112,128]{3,2,1,0:T(8,128)(2,1)} %get-tuple-element.951, s32[]{:T(128)S(6)} %sub.115), kind=kLoop, calls=%fused_computation.8.clone.1 | loop fusion | flops 4802560 | bytes 3325956 | tf_op jit(solution)/shard_map/while/body/eval_jaxpr/abl,bl->al/dot_general | solution.py:14
  91.9 3.0 %multiply_reduce_fusion.28 = f32[128,112]{0,1:T(8,128)S(1)} fusion(f32[128,112]{0,1:T(8,128)S(1)} %fusion.24, bf16[2,112,112,128]{3,2,1,0:T(8,128)(2,1)} %get-tuple-element.952, s32[]{:T(128)S(6)} %sub.115), kind=kLoop, calls=%fused_computation.7.clone.1 | loop fusion | flops 4802560 | bytes 3325956 | tf_op jit(solution)/shard_map/while
  94.9 0.1 copy.120
  95.0 0.1 copy.119
  95.1 3.0 %multiply_reduce_fusion.27 = f32[128,112]{0,1:T(8,128)S(1)} fusion(f32[128,112]{0,1:T(8,128)S(1)} %copy.119, bf16[2,112,112,128]{3,2,1,0:T(8,128)(2,1)} %get-tuple-element.951, s32[]{:T(128)S(6)} %sub.115), kind=kLoop, calls=%fused_computation.8.clone.1 | loop fusion | flops 4802560 | bytes 3325956 | tf_op jit(solution)/shard_map/while/body/eval_jaxpr/abl,bl->al/dot_general | solution.py:14
  98.1 3.0 %multiply_reduce_fusion.28 = f32[128,112]{0,1:T(8,128)S(1)} fusion(f32[128,112]{0,1:T(8,128)S(1)} %fusion.24, bf16[2,112,112,128]{3,2,1,0:T(8,128)(2,1)} %get-tuple-element.952, s32[]{:T(128)S(6)} %sub.115), kind=kLoop, calls=%fused_computation.7.clone.1 | loop fusion | flops 4802560 | bytes 3325956 | tf_op jit(solution)/shard_map/while
  101.1 0.1 copy.120
  101.2 1.5 collective-permute-start.3
  102.7 5.0 %collective-permute-done.3 = f32[112,128]{0,1:T(8,128)S(1)} collective-permute-done((f32[112,128]{0,1:T(8,128)S(1)}, f32[112,128]{0,1:T(8,128)S(1)}, u32[]{:S(2)}, u32[]{:S(2)}) %collective-permute-start.3) | collective-permute-done | bytes 57376 | tf_op jit(solution)/shard_map/ppermute | solution.py:10
  107.7 12.4 %while.105 = (s32[]{:T(128)}, f32[112,128]{0,1:T(8,128)S(1)}, f32[2,112,128]{2,1,0:T(8,128)S(1)}, bf16[2,112,112,128]{3,2,1,0:T(8,128)(2,1)}, bf16[2,112,112,128]{3,2,1,0:T(8,128)(2,1)}, /*index=5*/s32[]{:T(128)}) while((s32[]{:T(128)}, f32[112,128]{0,1:T(8,128)S(1)}, f32[2,112,128]{2,1,0:T(8,128)S(1)}, ...), condition=%wide.region_11.12_spmd, body=%wide.region_10.11_spmd.sunk | while | flops 9619459 | bytes 7053405 | solution.py:34
  107.8 3.0 %multiply_reduce_fusion.29 = f32[128,112]{0,1:T(8,128)S(1)} fusion(f32[128,112]{0,1:T(8,128)S(1)} %copy.121, bf16[2,112,112,128]{3,2,1,0:T(8,128)(2,1)} %get-tuple-element.969, s32[]{:T(128)S(6)} %sub.117), kind=kLoop, calls=%fused_computation.12.clone.1 | loop fusion | flops 4802560 | bytes 3325956 | tf_op jit(solution)/shard_map/while/body/eval_jaxpr/abl,bl->al/dot_general | solution.py:14
  110.8 3.0 %multiply_reduce_fusion.30 = f32[128,112]{0,1:T(8,128)S(1)} fusion(f32[128,112]{0,1:T(8,128)S(1)} %fusion.25, bf16[2,112,112,128]{3,2,1,0:T(8,128)(2,1)} %get-tuple-element.970, s32[]{:T(128)S(6)} %sub.117), kind=kLoop, calls=%fused_computation.11.clone.1 | loop fusion | flops 4802560 | bytes 3325956 | tf_op jit(solution)/shard_map/while
  113.8 0.1 copy.122
  113.9 0.1 copy.121
  114.0 3.0 %multiply_reduce_fusion.29 = f32[128,112]{0,1:T(8,128)S(1)} fusion(f32[128,112]{0,1:T(8,128)S(1)} %copy.121, bf16[2,112,112,128]{3,2,1,0:T(8,128)(2,1)} %get-tuple-element.969, s32[]{:T(128)S(6)} %sub.117), kind=kLoop, calls=%fused_computation.12.clone.1 | loop fusion | flops 4802560 | bytes 3325956 | tf_op jit(solution)/shard_map/while/body/eval_jaxpr/abl,bl->al/dot_general | solution.py:14
  117.0 3.0 %multiply_reduce_fusion.30 = f32[128,112]{0,1:T(8,128)S(1)} fusion(f32[128,112]{0,1:T(8,128)S(1)} %fusion.25, bf16[2,112,112,128]{3,2,1,0:T(8,128)(2,1)} %get-tuple-element.970, s32[]{:T(128)S(6)} %sub.117), kind=kLoop, calls=%fused_computation.11.clone.1 | loop fusion | flops 4802560 | bytes 3325956 | tf_op jit(solution)/shard_map/while
  120.0 0.1 copy.122
  120.1 1.3 collective-permute-start.4
  121.4 4.9 %collective-permute-done.4 = f32[112,128]{0,1:T(8,128)S(1)} collective-permute-done((f32[112,128]{0,1:T(8,128)S(1)}, f32[112,128]{0,1:T(8,128)S(1)}, u32[]{:S(2)}, u32[]{:S(2)}) %collective-permute-start.4) | collective-permute-done | bytes 57376 | tf_op jit(solution)/shard_map/ppermute | solution.py:10
  126.3 12.4 %while.106 = (s32[]{:T(128)}, f32[112,128]{0,1:T(8,128)S(1)}, f32[2,112,128]{2,1,0:T(8,128)S(1)}, bf16[2,112,112,128]{3,2,1,0:T(8,128)(2,1)}, bf16[2,112,112,128]{3,2,1,0:T(8,128)(2,1)}, /*index=5*/s32[]{:T(128)}) while((s32[]{:T(128)}, f32[112,128]{0,1:T(8,128)S(1)}, f32[2,112,128]{2,1,0:T(8,128)S(1)}, ...), condition=%wide.region_13.14_spmd, body=%wide.region_12.13_spmd.sunk | while | flops 9619459 | bytes 7053405 | solution.py:34
  126.4 3.0 %multiply_reduce_fusion.31 = f32[128,112]{0,1:T(8,128)S(1)} fusion(f32[128,112]{0,1:T(8,128)S(1)} %copy.123, bf16[2,112,112,128]{3,2,1,0:T(8,128)(2,1)} %get-tuple-element.987, s32[]{:T(128)S(6)} %sub.119), kind=kLoop, calls=%fused_computation.16.clone.1 | loop fusion | flops 4802560 | bytes 3325956 | tf_op jit(solution)/shard_map/while/body/eval_jaxpr/abl,bl->al/dot_general | solution.py:14
  129.4 3.0 %multiply_reduce_fusion.32 = f32[128,112]{0,1:T(8,128)S(1)} fusion(f32[128,112]{0,1:T(8,128)S(1)} %fusion.26, bf16[2,112,112,128]{3,2,1,0:T(8,128)(2,1)} %get-tuple-element.988, s32[]{:T(128)S(6)} %sub.119), kind=kLoop, calls=%fused_computation.15.clone.1 | loop fusion | flops 4802560 | bytes 3325956 | tf_op jit(solution)/shard_map/while
  132.4 0.1 copy.124
  132.5 0.1 copy.123
  132.6 3.0 %multiply_reduce_fusion.31 = f32[128,112]{0,1:T(8,128)S(1)} fusion(f32[128,112]{0,1:T(8,128)S(1)} %copy.123, bf16[2,112,112,128]{3,2,1,0:T(8,128)(2,1)} %get-tuple-element.987, s32[]{:T(128)S(6)} %sub.119), kind=kLoop, calls=%fused_computation.16.clone.1 | loop fusion | flops 4802560 | bytes 3325956 | tf_op jit(solution)/shard_map/while/body/eval_jaxpr/abl,bl->al/dot_general | solution.py:14
  135.6 3.0 %multiply_reduce_fusion.32 = f32[128,112]{0,1:T(8,128)S(1)} fusion(f32[128,112]{0,1:T(8,128)S(1)} %fusion.26, bf16[2,112,112,128]{3,2,1,0:T(8,128)(2,1)} %get-tuple-element.988, s32[]{:T(128)S(6)} %sub.119), kind=kLoop, calls=%fused_computation.15.clone.1 | loop fusion | flops 4802560 | bytes 3325956 | tf_op jit(solution)/shard_map/while
  138.6 0.1 copy.124
  138.8 1.3 collective-permute-start.5
  140.1 4.8 %collective-permute-done.5 = f32[112,128]{1,0:T(8,128)S(1)} collective-permute-done((f32[112,128]{1,0:T(8,128)S(1)}, f32[112,128]{1,0:T(8,128)S(1)}, u32[]{:S(2)}, u32[]{:S(2)}) %collective-permute-start.5) | collective-permute-done | bytes 57376 | tf_op jit(solution)/shard_map/ppermute | solution.py:10
  144.9 12.1 %while.107 = (s32[]{:T(128)}, f32[112,128]{1,0:T(8,128)S(1)}, f32[2,112,128]{2,1,0:T(8,128)S(1)}, f32[2,112,128]{2,1,0:T(8,128)S(1)}, bf16[2,112,112,128]{3,2,1,...) while((s32[]{:T(128)}, f32[112,128]{1,0:T(8,128)S(1)}, f32[2,112,128]{2,1,0:T(8,128)S(1)}, ...), condition=%wide.region_15.16_spmd, body=%wide.region_14.15_spmd.sunk | while | flops 9619459 | bytes 6938729 | solution.py:34
  144.9 3.0 %multiply_reduce_fusion.33 = f32[128,112]{0,1:T(8,128)S(1)} fusion(f32[128,112]{0,1:T(8,128)S(1)} %bitcast.219, bf16[2,112,112,128]{3,2,1,0:T(8,128)(2,1)} %get-tuple-element.1008, s32[]{:T(128)S(6)} %sub.121), kind=kLoop, calls=%fused_computation.20.clone.1 | loop fusion | flops 4802560 | bytes 3325956 | tf_op jit(solution)/shard_map/while/body/eval_jaxpr/abl,bl->al/dot_general | solution.py:14
  147.9 3.0 %multiply_reduce_fusion.34 = f32[128,112]{0,1:T(8,128)S(1)} fusion(f32[128,112]{0,1:T(8,128)S(1)} %fusion.27, bf16[2,112,112,128]{3,2,1,0:T(8,128)(2,1)} %get-tuple-element.1009, s32[]{:T(128)S(6)} %sub.121), kind=kLoop, calls=%fused_computation.19.clone.1 | loop fusion | flops 4802560 | bytes 3325956 | tf_op jit(solution)/shard_map/while/body/eval_jaxpr/abl,bl->al/dot_general | solution.py:14
  150.9 3.0 %multiply_reduce_fusion.33 = f32[128,112]{0,1:T(8,128)S(1)} fusion(f32[128,112]{0,1:T(8,128)S(1)} %bitcast.219, bf16[2,112,112,128]{3,2,1,0:T(8,128)(2,1)} %get-tuple-element.1008, s32[]{:T(128)S(6)} %sub.121), kind=kLoop, calls=%fused_computation.20.clone.1 | loop fusion | flops 4802560 | bytes 3325956 | tf_op jit(solution)/shard_map/while/body/eval_jaxpr/abl,bl->al/dot_general | solution.py:14
  153.9 3.0 %multiply_reduce_fusion.34 = f32[128,112]{0,1:T(8,128)S(1)} fusion(f32[128,112]{0,1:T(8,128)S(1)} %fusion.27, bf16[2,112,112,128]{3,2,1,0:T(8,128)(2,1)} %get-tuple-element.1009, s32[]{:T(128)S(6)} %sub.121), kind=kLoop, calls=%fused_computation.19.clone.1 | loop fusion | flops 4802560 | bytes 3325956 | tf_op jit(solution)/shard_map/while/body/eval_jaxpr/abl,bl->al/dot_general | solution.py:14
  156.9 0.6 copy-done.1
  (37 shorter events, 0.7 us)
Async XLA Ops:
  0.0 2.3 %copy-start = (f32[2,112,128]{2,1,0:T(8,128)S(1)}, f32[2,112,128]{2,1,0:T(8,128)}, u32[]{:S(2)}) copy-start(f32[2,112,128]{2,1,0:T(8,128)} %param.29) | copy-start | bytes 344068
  0.0 13.4 %copy-start.3 = (s32[1,32,64]{2,1,0:T(8,128)S(1)}, s32[1,32,64]{2,1,0:T(8,128)}, u32[]{:S(2)}) copy-start(s32[1,32,64]{2,1,0:T(8,128)} %param.32) | copy-start | bytes 24580
  3.2 41.8 %copy-start.2 = (f32[2,112,128]{2,1,0:T(8,128)S(1)}, f32[2,112,128]{2,1,0:T(8,128)}, u32[]{:S(2)}) copy-start(f32[2,112,128]{2,1,0:T(8,128)} %param.28) | copy-start | bytes 344068
  5.1 37.3 %all-to-all-start = ((f32[224,32,64]{0,2,1:T(8,128)}), f32[224,32,64]{0,2,1:T(8,128)}, u32[]{:S(2)}, u32[]{:S(2)}) async-start(f32[224,32,64]{0,2,1:T(8,128)} %bitcast.70), calls=%async_computation | async-start | bytes 4194304 | tf_op jit(solution)/shard_map/all_to_all | solution.py:58
  53.2 5.3 %collective-permute-start = (f32[112,128]{1,0:T(8,128)S(1)}, f32[112,128]{1,0:T(8,128)S(1)}, u32[]{:S(2)}, u32[]{:S(2)}) collective-permute-start(f32[112,128]{1,0:T(8,128)S(1)} %get-tuple-element.529), channel_id=1, source_target_pairs={{0,32},{32,64},{64,96},{1,33},{33,65},{65,97},{2,34},{34,66},{66,9... | collective-permute-start | bytes 172040 | tf_op jit(solution)/shard_map/ppermute | solution.py:10
  64.5 6.1 %collective-permute-start.1 = (f32[112,128]{1,0:T(8,128)S(1)}, f32[112,128]{1,0:T(8,128)S(1)}, u32[]{:S(2)}, u32[]{:S(2)}) collective-permute-start(f32[112,128]{1,0:T(8,128)S(1)} %get-tuple-element.530), channel_id=1, source_target_pairs={{0,32},{32,64},{64,96},{1,33},{33,65},{65,97},{2,34},{34,66},{66,9... | collective-permute-start | bytes 172040 | tf_op jit(solution)/shard_map/ppermute | solution.py:10
  76.6 6.1 %collective-permute-start.2 = (f32[112,128]{1,0:T(8,128)S(1)}, f32[112,128]{1,0:T(8,128)S(1)}, u32[]{:S(2)}, u32[]{:S(2)}) collective-permute-start(f32[112,128]{1,0:T(8,128)S(1)} %get-tuple-element.531), channel_id=1, source_target_pairs={{0,32},{32,64},{64,96},{1,33},{33,65},{65,97},{2,34},{34,66},{66,9... | collective-permute-start | bytes 172040 | tf_op jit(solution)/shard_map/ppermute | solution.py:10
  101.2 6.5 %collective-permute-start.3 = (f32[112,128]{0,1:T(8,128)S(1)}, f32[112,128]{0,1:T(8,128)S(1)}, u32[]{:S(2)}, u32[]{:S(2)}) collective-permute-start(f32[112,128]{0,1:T(8,128)S(1)} %get-tuple-element.533), channel_id=1, source_target_pairs={{32,0},{64,32},{96,64},{33,1},{65,33},{97,65},{34,2},{66,34},{98,6... | collective-permute-start | bytes 172040 | tf_op jit(solution)/shard_map/ppermute | solution.py:10
  120.1 6.2 %collective-permute-start.4 = (f32[112,128]{0,1:T(8,128)S(1)}, f32[112,128]{0,1:T(8,128)S(1)}, u32[]{:S(2)}, u32[]{:S(2)}) collective-permute-start(f32[112,128]{0,1:T(8,128)S(1)} %get-tuple-element.534), channel_id=1, source_target_pairs={{32,0},{64,32},{96,64},{33,1},{65,33},{97,65},{34,2},{66,34},{98,6... | collective-permute-start | bytes 172040 | tf_op jit(solution)/shard_map/ppermute | solution.py:10
  138.8 6.1 %collective-permute-start.5 = (f32[112,128]{1,0:T(8,128)S(1)}, f32[112,128]{1,0:T(8,128)S(1)}, u32[]{:S(2)}, u32[]{:S(2)}) collective-permute-start(f32[112,128]{1,0:T(8,128)S(1)} %copy.13), channel_id=1, source_target_pairs={{32,0},{64,32},{96,64},{33,1},{65,33},{97,65},{34,2},{66,34},{98,6... | collective-permute-start | bytes 172040 | tf_op jit(solution)/shard_map/ppermute | solution.py:10
  156.9 0.6 copy-start.1
where the time goes:
time: 159 us; the launch traced here: 158 us
  other arithmetic  72.7 us (46%)
  waiting for transfers between devices  48.9 us (31%)
  starting transfers between devices  24.4 us (15%)
  local copies, waits for them, and re-layouts  7.23 us (5%)
  matrix products  3 us (2%)
    dot_general x18, other arithmetic, matvec(): jnp.einsum('abl,bl->al', block.astype(jnp.float32), vec, precision=lax.Pr...  53.7 us
    all_to_all x1, waiting for transfers between devices, local(): lax.all_to_all(outgoing, 'span', split_axis=1, concat_axis=1, tiled=True)  28.8 us
    ppermute x6, waiting for transfers between devices, from_behind(): lax.ppermute(value, axis, [(source, source + steps) for source in range(f...  20.1 us
    while x16, other arithmetic  18 us
    ppermute x6, starting transfers between devices, from_behind(): lax.ppermute(value, axis, [(source, source + steps) for source in range(f...  16 us
    all_to_all x1, starting transfers between devices, local(): lax.all_to_all(outgoing, 'span', split_axis=1, concat_axis=1, tiled=True)  8.38 us
  transfers between devices with their start and end apart: 7, of which 7 were waited for; matrix products, arithmetic and copies ran while one was open for 0% of the time, Pallas kernels for 0%

commit v1 on v0

v1 whole, which is shorter than its diff:
```python
import functools

import jax
import jax.numpy as jnp
from jax import lax
from jax.experimental import pallas as pl
from jax.experimental.pallas import tpu as pltpu
from jax.sharding import PartitionSpec as P

MESH = pl.DeviceIdType.MESH
BF16 = jnp.bfloat16
F32 = jnp.float32
I32 = jnp.int32

NC = 112
LD = 128
SLOTS = 64
CH = 4
CL = LD // CH
GR = NC // CH
CR = 32


def iota(shape, dim):
    return lax.broadcasted_iota(I32, shape, dim)


def fold(rows):
    sub = iota((8, LD), 0)
    for d in (1, 2, 4):
        low = (sub & d) == 0
        rows = [
            jnp.where(low, a, b) + pltpu.roll(jnp.where(low, b, a), d, 0)
            for a, b in zip(rows[0::2], rows[1::2])
        ]
    return rows[0]


def matvec(mat_ref, vec):
    def row(j):
        return jnp.sum((mat_ref[j] * vec).reshape(NC // 8, 8, LD), axis=0)

    rows = [row(j) for j in range(GR)]
    tiles = [fold(rows[8 * t : 8 * t + 8]) for t in range(3)]
    return tiles + [fold(rows[24:28] + rows[24:28])]


def expand(tiles):
    lane = iota((8, LD), 1)
    odd = (lane // CL) % 2 == 1
    upper = lane >= 2 * CL
    top = iota((8, LD), 0) < 4
    out = [None] * 14
    for t in range(4):
        turned = [tiles[t]] + [pltpu.roll(tiles[t], CL * d, 1) for d in (1, 2, 3)]
        one = [jnp.where(odd, turned[(k + 1) % 4], turned[k]) for k in range(4)]
        two = [jnp.where(upper, one[(k + 2) % 4], one[k]) for k in range(4)]
        group = [two[(-q) % 4] for q in range(4)]
        if t < 3:
            out[4 * t : 4 * t + 4] = group
        else:
            out[12] = jnp.where(top, group[0], group[1])
            out[13] = jnp.where(top, group[2], group[3])
    return jnp.concatenate(out, 0)


def pack(ref, cell, chunk):
    group = iota((8, LD), 1) // CL
    tiles = []
    for t in range(4):
        out = None
        for q in range(4):
            tile = 4 * t + q if t < 3 else 12 + q // 2
            turned = pltpu.roll(ref[cell, pl.ds(8 * tile, 8), :], lax.rem(CL * (q - chunk) + 2 * LD, LD), 1)
            out = turned if out is None else jnp.where(group == q, turned, out)
        tiles.append(out)
    return tiles


def load_tiles(ref, *at):
    return [ref[at + (pl.ds(8 * t, 8), slice(None))] for t in range(4)]


def store_tiles(ref, tiles, *at):
    for t in range(4):
        ref[at + (pl.ds(8 * t, 8), slice(None))] = tiles[t]


def kernel(
    low_hbm, inv_hbm, upp_hbm, res_hbm, prev_hbm, sl_hbm, sc_hbm, rl_hbm, act_hbm,
    out_ref,
    stage, mats, perm, prev, res, sl, sc, rl, act,
    si, ri, gsi, gri, gp, pick, land, picked, part, pbuf,
    rhs, yin, xin, yc, xc, edge,
    stage_sem, in_sem, si_ss, si_rs, ri_ss, ri_rs, gp_ss, gp_rs, pt_ss, pt_rs, y_ss, y_rs, x_ss, x_rs,
):
    w = lax.axis_index("wall")
    span = lax.axis_index("span")
    x, z, c = span // 8, (span // 2) % 4, span % 2

    def dev(dx, dz, core):
        return (w, (dx * 4 + dz) * 2 + core)

    ring = [lambda v, d=d: lax.rem(v + d, 4) for d in (1, 2, 3)]

    smalls = [
        pltpu.make_async_copy(sl_hbm.at[0], sl, in_sem.at[0]),
        pltpu.make_async_copy(sc_hbm, sc, in_sem.at[1]),
        pltpu.make_async_copy(rl_hbm.at[0], rl, in_sem.at[2]),
        pltpu.make_async_copy(act_hbm, act, in_sem.at[3]),
        pltpu.make_async_copy(prev_hbm, prev, in_sem.at[4]),
        pltpu.make_async_copy(res_hbm, res, in_sem.at[5]),
    ]
    for copy in smalls:
        copy.start()
    sources = [low_hbm.at[0], low_hbm.at[1], upp_hbm.at[1], inv_hbm.at[1], upp_hbm.at[0], inv_hbm.at[0]]

    def stage_copy(m):
        return pltpu.make_async_copy(sources[m], stage.at[m % 3], stage_sem.at[m])

    for m in range(3):
        stage_copy(m).start()

    barrier = pltpu.get_barrier_semaphore()
    partners = [dev(turn(x), z, core) for turn in ring for core in (0, 1)]
    partners += [dev(x, turn(z), core) for turn in ring for core in (0, 1)]
    partners += [dev(x, z, 1 - c), (lax.rem(w + 1, 4), span), (lax.rem(w + 3, 4), span)]
    for partner in partners:
        pl.semaphore_signal(barrier, inc=1, device_id=partner, device_id_type=MESH)

    k = iota((512, 512), 0)
    n = iota((512, 512), 1)
    moved = (k % LD) // CL * LD + k // LD * CL + k % CL
    perm[...] = (moved == n).astype(F32).astype(BF16)

    for copy in smalls[:4]:
        copy.wait()
    active = act[0]
    diag = iota((32, 32), 0) == iota((32, 32), 1)
    count = jnp.sum(jnp.where(diag, sc[...].astype(F32), 0.0), axis=1, keepdims=True)
    lines = sl[...]
    used = (iota((32, SLOTS), 1).astype(F32) < count) & (lines < active)
    lines = jnp.where(used, lines, -1)
    recv = rl[...]

    def z_rows(values, at):
        return jnp.concatenate([values[8 * g + 2 * at : 8 * g + 2 * at + 2] for g in range(4)], 0)

    for g in range(4):
        for kind, rows in ((0, lines[8 * g : 8 * g + 8]), (4, z_rows(lines, g))):
            si[kind + g, 0:4, :] = jnp.concatenate([rows[0:4], rows[4:8]], 1)
            si[kind + g, 4:8, :] = jnp.zeros((4, LD), I32)
        for kind, rows in ((0, recv[8 * g : 8 * g + 8]), (4, z_rows(recv, g))):
            ri[kind + g] = jnp.concatenate([rows, rows], 1)

    other = 1 - c
    sends = [(dev(turn(x), z, 0), 0, turn(x), 2 * x + c) for turn in ring]
    sends += [(dev(x, turn(z), 1), 1, 4 + turn(z), 2 * z + c) for turn in ring]
    sends += [(dev(x, z, other), other, c * x + other * (4 + z), 2 * (c * x + other * z) + c)]
    marks = [(dev(x, turn(z), 0), 4 + turn(z), 2 * z + c) for turn in ring]
    marks += [(dev(turn(x), z, 1), turn(x), 2 * x + c) for turn in ring]
    marks += [(dev(x, z, other), other * x + c * (4 + z), 2 * (other * x + c * z) + c)]
    own_tile = other * x + c * (4 + z)
    own_slot = 2 * (other * x + c * z) + c
    own_mark_tile = c * x + other * (4 + z)
    own_mark = 2 * (c * x + other * z) + c

    def remote(src, dst, send_sem, recv_sem, device):
        return pltpu.make_async_remote_copy(
            src_ref=src, dst_ref=dst, send_sem=send_sem, recv_sem=recv_sem,
            device_id=device, device_id_type=MESH,
        )

    pl.semaphore_wait(barrier, len(partners))
    started = []
    for i, (device, _, tile, slot) in enumerate(sends):
        started.append(remote(si.at[tile], gsi.at[slot], si_ss.at[i], si_rs.at[slot], device))
        started[-1].start()
    for i, (device, tile, slot) in enumerate(marks):
        started.append(remote(ri.at[tile], gri.at[slot], ri_ss.at[i], ri_rs.at[slot], device))
        started[-1].start()
    smalls[4].wait()
    for i, (device, cell, _, slot) in enumerate(sends):
        started.append(remote(prev.at[cell], gp.at[slot], gp_ss.at[i], gp_rs.at[slot], device))
        started[-1].start()
    gsi[own_slot] = si[own_tile]
    gri[own_mark] = ri[own_mark_tile]
    gp[own_slot] = prev[c]

    def relayout(m):
        stage_copy(m).wait()
        source = stage.at[m % 3]
        blocks = []
        for q in range(CH):
            rows = [source[pl.ds(32 * t + 8 * q, 8)] for t in range(3)] + [source[pl.ds(96 + 4 * q, 4)]]
            blocks.append(jnp.concatenate(rows, 0).reshape(GR * NC, LD))
        turned = jnp.dot(jnp.concatenate(blocks, 1), perm[...], preferred_element_type=F32)
        for chunk in range(CH):
            mats[m, chunk] = turned[:, LD * chunk : LD * chunk + LD].reshape(GR, NC, LD)
        if m + 3 < 6:
            stage_copy(m + 3).start()

    relayout(0)

    def arrived(src, dst, recv_sem, own):
        for i in range(8):
            @pl.when(i != own)
            def _():
                remote(src, dst.at[i], si_ss.at[0], recv_sem.at[i], dev(x, z, other)).wait_recv()

    arrived(si.at[0], gsi, si_rs, own_slot)
    arrived(ri.at[0], gri, ri_rs, own_mark)
    low_lanes = iota((8, LD), 1) < SLOTS
    for s in range(8):
        for p in range(4):
            hot = iota((LD, LD), 0) == gsi[s, pl.ds(p, 1), :]
            pick[s, :, LD * p : LD * p + LD] = hot.astype(F32).astype(BF16)
    for p in range(4):
        target = jnp.where(low_lanes, gri[p], gri[p + 4] + LD)
        for s in range(8):
            hot = iota((2 * LD, LD), 0) == target[s : s + 1]
            land[p, :, LD * s : LD * s + LD] = hot.astype(F32).astype(BF16)

    arrived(prev.at[0], gp, gp_rs, own_slot)
    for s in range(8):
        value = gp[s]
        high = value.astype(BF16)
        rest = (value - high.astype(F32)).astype(BF16)
        got = jnp.dot(jnp.concatenate([high, rest], 0), pick[s], preferred_element_type=F32).astype(BF16)
        for p in range(4):
            picked[p, :, LD * s : LD * s + LD] = got[:, LD * p : LD * p + LD]
    place = other * z + c * x
    for p in range(4):
        total = lax.dot_general(picked[p], land[p], (((1,), (1,)), ((), ())), preferred_element_type=F32)
        total = total[:NC] + total[NC:]
        for h in range(2):
            part[p + 4 * h] = total[:, LD * h : LD * h + LD]
        for j in (p, p + 4):
            device = (w, other * ((x * 4 + j // 2) * 2 + j % 2) + c * (((j // 2) * 4 + z) * 2 + j % 2))

            @pl.when(j != own_mark_slot(x, z, c))
            def _():
                remote(part.at[j], pbuf.at[c, place], pt_ss.at[j], pt_rs.at[c, place], device).start()

    mine = own_mark_slot(x, z, c)
    pbuf[c, place] = part[mine]

    relayout(1)
    relayout(2)
    smalls[5].wait()

    @pl.when((w == 0) | (w == 3))
    def _():
        zero = jnp.zeros((NC, LD), F32)
        which = jnp.where(w == 0, 0, 2)

        def one(chunk, carry):
            store_tiles(edge, matvec(mats.at[which, chunk], zero), chunk)
            return carry

        lax.fori_loop(0, CH, one, 0)

    for cell in range(2):
        for slot in range(4):
            @pl.when((c != cell) | (place != slot))
            def _():
                remote(part.at[0], pbuf.at[cell, slot], pt_ss.at[0], pt_rs.at[cell, slot], dev(x, z, other)).wait_recv()

    live = (iota((NC, LD), 1) < active).astype(F32)
    for cell in range(2):
        coupling = (pbuf[cell, 0] + pbuf[cell, 1]) + (pbuf[cell, 2] + pbuf[cell, 3])
        rhs[cell] = (res[cell] - coupling) * live

    above = (lax.rem(w + 1, 4), span)
    below = (lax.rem(w + 3, 4), span)

    def y_copy(chunk):
        return remote(yc.at[1, chunk], yin.at[chunk], y_ss.at[chunk], y_rs.at[chunk], above)

    def x_copy(chunk):
        return remote(xc.at[chunk], xin.at[chunk], x_ss.at[chunk], x_rs.at[chunk], below)

    def minus(a, b):
        return [i - j for i, j in zip(a, b)]

    def forward(chunk):
        @pl.when(w > 0)
        def _():
            y_copy(chunk).wait_recv()
            store_tiles(yc, matvec(mats.at[0, chunk], expand(load_tiles(yin, chunk))), 0, chunk)

        @pl.when(w == 0)
        def _():
            store_tiles(yc, load_tiles(edge, chunk), 0, chunk)

        first = minus(pack(rhs, 0, chunk), load_tiles(yc, 0, chunk))
        store_tiles(yc, first, 0, chunk)
        second = minus(pack(rhs, 1, chunk), matvec(mats.at[1, chunk], expand(first)))
        store_tiles(yc, second, 1, chunk)

        @pl.when(w < 3)
        def _():
            y_copy(chunk).start()

    def backward(chunk):
        @pl.when(w < 3)
        def _():
            x_copy(chunk).wait_recv()
            store_tiles(xc, matvec(mats.at[2, chunk], expand(load_tiles(xin, chunk))), chunk)

        @pl.when(w == 3)
        def _():
            store_tiles(xc, load_tiles(edge, chunk), chunk)

        here = iota((NC, LD), 1) // CL == chunk
        right = minus(load_tiles(yc, 1, chunk), load_tiles(xc, chunk))
        value = expand(matvec(mats.at[3, chunk], expand(right)))
        out_ref[1] = jnp.where(here, value, out_ref[1])
        right = minus(load_tiles(yc, 0, chunk), matvec(mats.at[4, chunk], value))
        last = matvec(mats.at[5, chunk], expand(right))
        store_tiles(xc, last, chunk)

        @pl.when(w > 0)
        def _():
            x_copy(chunk).start()

        out_ref[0] = jnp.where(here, expand(last), out_ref[0])

    out_ref[...] = jnp.zeros((2, NC, LD), F32)

    def step(t, carry):
        @pl.when(t == jnp.where(w == 3, 0, CH))
        def _():
            for m in (3, 4, 5):
                relayout(m)

        is_forward = jnp.where(w == 3, t % 2 == 0, t < CH)
        chunk = jnp.where(w == 3, t // 2, t % CH)

        @pl.when(is_forward)
        def _():
            forward(chunk)

        @pl.when(jnp.logical_not(is_forward))
        def _():
            backward(chunk)

        return carry

    lax.fori_loop(0, 2 * CH, step, 0)

    for copy in started:
        copy.wait_send()
    for j in range(8):
        @pl.when(j != mine)
        def _():
            remote(part.at[j], pbuf.at[0, 0], pt_ss.at[j], pt_rs.at[0, 0], dev(x, z, other)).wait_send()

    @pl.when(w < 3)
    def _():
        for chunk in range(CH):
            y_copy(chunk).wait_send()

    @pl.when(w > 0)
    def _():
        for chunk in range(CH):
            x_copy(chunk).wait_send()


def own_mark_slot(x, z, c):
    return 2 * ((1 - c) * z + c * x) + c


def local(*args):
    dma = pltpu.SemaphoreType.DMA
    scratch = [
        pltpu.VMEM((3, NC, NC, LD), BF16),
        pltpu.VMEM((6, CH, GR, NC, LD), F32),
        pltpu.VMEM((4 * LD, 4 * LD), BF16),
        pltpu.VMEM((2, NC, LD), F32),
        pltpu.VMEM((2, NC, LD), F32),
        pltpu.VMEM((32, SLOTS), I32),
        pltpu.VMEM((1, 32), I32),
        pltpu.VMEM((32, SLOTS), I32),
        pltpu.SMEM((1,), I32),
        pltpu.VMEM((8, 8, LD), I32),
        pltpu.VMEM((8, 8, LD), I32),
        pltpu.VMEM((8, 8, LD), I32),
        pltpu.VMEM((8, 8, LD), I32),
        pltpu.VMEM((8, NC, LD), F32),
        pltpu.VMEM((8, LD, 4 * LD), BF16),
        pltpu.VMEM((4, 2 * LD, 8 * LD), BF16),
        pltpu.VMEM((4, 2 * NC, 8 * LD), BF16),
        pltpu.VMEM((8, NC, LD), F32),
        pltpu.VMEM((2, 4, NC, LD), F32),
        pltpu.VMEM((2, NC, LD), F32),
        pltpu.VMEM((CH, CR, LD), F32),
        pltpu.VMEM((CH, CR, LD), F32),
        pltpu.VMEM((2, CH, CR, LD), F32),
        pltpu.VMEM((CH, CR, LD), F32),
        pltpu.VMEM((CH, CR, LD), F32),
        dma((6,)), dma((6,)),
        dma((7,)), dma((8,)), dma((7,)), dma((8,)), dma((7,)), dma((8,)),
        dma((8,)), dma((2, 4)), dma((CH,)), dma((CH,)), dma((CH,)), dma((CH,)),
    ]
    return pl.pallas_call(
        kernel,
        out_shape=jax.ShapeDtypeStruct((2, NC, LD), F32),
        in_specs=[pl.BlockSpec(memory_space=pl.ANY)] * 9,
        out_specs=pl.BlockSpec(memory_space=pltpu.VMEM),
        scratch_shapes=scratch,
        compiler_params=pltpu.CompilerParams(
            collective_id=0, has_side_effects=True, vmem_limit_bytes=62 * 2**20
        ),
        name="relax",
    )(*args)


def solution(mesh):
    return jax.shard_map(
        local,
        mesh=mesh,
        in_specs=(
            P("wall", None, None, "span"),
            P("wall", None, None, "span"),
            P("wall", None, None, "span"),
            P("wall", None, "span"),
            P("wall", None, "span"),
            P("span", None, None),
            P("span", None),
            P("span", None, None),
            P("span"),
        ),
        out_specs=P("wall", None, "span"),
        check_vma=False,
    )
```

time: 159 us -> 46 us (0.29)
  other arithmetic: 72.7 us -> 0 us
  waiting for transfers between devices: 48.9 us -> 0 us
  Pallas kernels: 0 us -> 43.6 us
  starting transfers between devices: 24.4 us -> 0 us
  local copies, waits for them, and re-layouts: 7.23 us -> 1.55 us
  matrix products: 3 us -> 0 us
    dot_general x18 -> x0, other arithmetic: 53.7 us -> none  [matvec(): jnp.einsum('abl,bl->al', block.astype(jnp.float32), vec, precision=lax.Pr...]
    pallas_call x0 -> x1, Pallas kernels: none -> 43.6 us  [local(): pl.pallas_call(kernel, out_shape=jax.ShapeDtypeStruct((2, NC, LD), F32),...]
    all_to_all x1 -> x0, waiting for transfers between devices: 28.8 us -> none  [local(): lax.all_to_all(outgoing, 'span', split_axis=1, concat_axis=1, tiled=True)]
    ppermute x6 -> x0, waiting for transfers between devices: 20.1 us -> none  [from_behind(): lax.ppermute(value, axis, [(source, source + steps) for source in range(f...]
    while x16 -> x0, other arithmetic: 18 us -> none
    ppermute x6 -> x0, starting transfers between devices: 16 us -> none  [from_behind(): lax.ppermute(value, axis, [(source, source + steps) for source in range(f...]
    all_to_all x1 -> x0, starting transfers between devices: 8.38 us -> none  [local(): lax.all_to_all(outgoing, 'span', split_axis=1, concat_axis=1, tiled=True)]
    dot_general x8 -> x0, local copies, waits for them, and re-layouts: 4.97 us -> none  [the longest x1 2.63 us: local(): jnp.dot(incoming.reshape(cells * width, spans * slot_count), landing, pre...]
  transfers between devices with their start and end apart: 7 -> 0, of which waited for: 7 -> 0; matrix products, arithmetic and copies ran while one was open for 0% -> 0% of each run, Pallas kernels for 0% -> 0%
where the time goes in v1:
time: 46 us; the launch traced here: 45.8 us
  Pallas kernels  43.6 us (95%)
  local copies, waits for them, and re-layouts  1.55 us (3%)
  between operations  0.66 us (1%)
    pallas_call x1, Pallas kernels, local(): pl.pallas_call(kernel, out_shape=jax.ShapeDtypeStruct((2, NC, LD), F32),...  43.6 us
    unnamed x1, local copies, waits for them, and re-layouts  1.55 us

profile of v1, /device:TPU:0, one launch (start us, length us, event | category | flops | bytes accessed | tf_op | source)
XLA Modules:
  0.0 45.8 jit_solution(9945216447906953916)
XLA Ops:
  0.7 43.6 %relax.1 = f32[2,112,128]{2,1,0:T(8,128)} custom-call(bf16[2,112,112,128]{3,2,1,0:T(8,128)(2,1)} %low_hbm.1, bf16[2,112,112,128]{3,2,1,0:T(8,128)(2,1)} %inv_hbm.1, bf16[2,112,112,128]{3,2,1,0:T(8,128)(2,1)} %upp_hbm.1, f32[2,112,128]{2,1,0:T(8,128)} %res_hbm.1, f32[2,112,128]{2,1,0:T(8,128)} %prev_hbm.1, s32[1,32,64]{2,1,0:T(8,128)} %sl_hbm.1, ...), custom_call_target="tpu_custom_call" | custom-call | tf_op jit(solution)/shard_map/relax/pallas_call | solution.py:406
  44.3 1.6 %copy.12 = f32[2,112,128]{2,1,0:T(8,128)} copy(f32[2,112,128]{2,1,0:T(8,128)} %relax.1) | data formatting | bytes 229376

commit v2 on v1

--- a/solution.py
+++ b/solution.py
@@ -47,7 +47,7 @@
 
 def expand(tiles):
     lane = iota((8, LD), 1)
-    odd = (lane // CL) % 2 == 1
+    odd = (lane & CL) != 0
     upper = lane >= 2 * CL
     top = iota((8, LD), 0) < 4
     out = [None] * 14
@@ -65,15 +65,18 @@
 
 
 def pack(ref, cell, chunk):
-    group = iota((8, LD), 1) // CL
+    lane = iota((8, LD), 1)
+    odd = (lane & CL) != 0
+    upper = lane >= 2 * CL
     tiles = []
     for t in range(4):
-        out = None
+        turned = []
         for q in range(4):
             tile = 4 * t + q if t < 3 else 12 + q // 2
-            turned = pltpu.roll(ref[cell, pl.ds(8 * tile, 8), :], lax.rem(CL * (q - chunk) + 2 * LD, LD), 1)
-            out = turned if out is None else jnp.where(group == q, turned, out)
-        tiles.append(out)
+            turned.append(pltpu.roll(ref[cell, pl.ds(8 * tile, 8), :], lax.rem(CL * (q - chunk) + 2 * LD, LD), 1))
+        low = jnp.where(odd, turned[1], turned[0])
+        high = jnp.where(odd, turned[3], turned[2])
+        tiles.append(jnp.where(upper, high, low))
     return tiles
 
 
@@ -90,8 +93,8 @@
     low_hbm, inv_hbm, upp_hbm, res_hbm, prev_hbm, sl_hbm, sc_hbm, rl_hbm, act_hbm,
     out_ref,
     stage, mats, perm, prev, res, sl, sc, rl, act,
-    si, ri, gsi, gri, gp, pick, land, picked, part, pbuf,
-    rhs, yin, xin, yc, xc, edge,
+    si, ri, gsi, gri, gp, pick, land, moves, parts, part, pbuf,
+    rhs, packed, yin, xin, yc, xc, upper_x, edge,
     stage_sem, in_sem, si_ss, si_rs, ri_ss, ri_rs, gp_ss, gp_rs, pt_ss, pt_rs, y_ss, y_rs, x_ss, x_rs,
 ):
     w = lax.axis_index("wall")
@@ -101,7 +104,7 @@
     def dev(dx, dz, core):
         return (w, (dx * 4 + dz) * 2 + core)
 
-    ring = [lambda v, d=d: lax.rem(v + d, 4) for d in (1, 2, 3)]
+    ring = [lambda v, d=d: lax.rem(v + d, 4) for d in (2, 1, 3)]
 
     smalls = [
         pltpu.make_async_copy(sl_hbm.at[0], sl, in_sem.at[0]),
@@ -128,10 +131,12 @@
     for partner in partners:
         pl.semaphore_signal(barrier, inc=1, device_id=partner, device_id_type=MESH)
 
-    k = iota((512, 512), 0)
-    n = iota((512, 512), 1)
-    moved = (k % LD) // CL * LD + k // LD * CL + k % CL
-    perm[...] = (moved == n).astype(F32).astype(BF16)
+    chunk_bits, line_bits = LD.bit_length() - 1, CL.bit_length() - 1
+    n = iota((LD, 512), 1)
+    k = iota((LD, 512), 0)
+    for q in range(CH):
+        moved = ((k >> line_bits) << chunk_bits) + q * CL + (k & (CL - 1))
+        perm[LD * q : LD * q + LD, :] = (moved == n).astype(F32).astype(BF16)
 
     for copy in smalls[:4]:
         copy.wait()
@@ -221,17 +226,23 @@
             hot = iota((2 * LD, LD), 0) == target[s : s + 1]
             land[p, :, LD * s : LD * s + LD] = hot.astype(F32).astype(BF16)
 
+    for p in range(4):
+        for s in range(8):
+            times = lax.dot_general(
+                pick[s, :, LD * p : LD * p + LD], land[p, :, LD * s : LD * s + LD],
+                (((1,), (1,)), ((), ())), preferred_element_type=F32,
+            )
+            moves[p, LD * s : LD * s + LD, :] = times.astype(BF16)
+
     arrived(prev.at[0], gp, gp_rs, own_slot)
     for s in range(8):
         value = gp[s]
         high = value.astype(BF16)
-        rest = (value - high.astype(F32)).astype(BF16)
-        got = jnp.dot(jnp.concatenate([high, rest], 0), pick[s], preferred_element_type=F32).astype(BF16)
-        for p in range(4):
-            picked[p, :, LD * s : LD * s + LD] = got[:, LD * p : LD * p + LD]
+        parts[0:NC, LD * s : LD * s + LD] = high
+        parts[NC : 2 * NC, LD * s : LD * s + LD] = (value - high.astype(F32)).astype(BF16)
     place = other * z + c * x
     for p in range(4):
-        total = lax.dot_general(picked[p], land[p], (((1,), (1,)), ((), ())), preferred_element_type=F32)
+        total = jnp.dot(parts[...], moves[p], preferred_element_type=F32)
         total = total[:NC] + total[NC:]
         for h in range(2):
             part[p + 4 * h] = total[:, LD * h : LD * h + LD]
@@ -293,9 +304,9 @@
         def _():
             store_tiles(yc, load_tiles(edge, chunk), 0, chunk)
 
-        first = minus(pack(rhs, 0, chunk), load_tiles(yc, 0, chunk))
+        first = minus(load_tiles(packed, 0, chunk), load_tiles(yc, 0, chunk))
         store_tiles(yc, first, 0, chunk)
-        second = minus(pack(rhs, 1, chunk), matvec(mats.at[1, chunk], expand(first)))
+        second = minus(load_tiles(packed, 1, chunk), matvec(mats.at[1, chunk], expand(first)))
         store_tiles(yc, second, 1, chunk)
 
         @pl.when(w < 3)
@@ -312,19 +323,26 @@
         def _():
             store_tiles(xc, load_tiles(edge, chunk), chunk)
 
-        here = iota((NC, LD), 1) // CL == chunk
         right = minus(load_tiles(yc, 1, chunk), load_tiles(xc, chunk))
-        value = expand(matvec(mats.at[3, chunk], expand(right)))
-        out_ref[1] = jnp.where(here, value, out_ref[1])
-        right = minus(load_tiles(yc, 0, chunk), matvec(mats.at[4, chunk], value))
-        last = matvec(mats.at[5, chunk], expand(right))
-        store_tiles(xc, last, chunk)
+        value = matvec(mats.at[3, chunk], expand(right))
+        store_tiles(upper_x, value, chunk)
+        right = minus(load_tiles(yc, 0, chunk), matvec(mats.at[4, chunk], expand(value)))
+        store_tiles(xc, matvec(mats.at[5, chunk], expand(right)), chunk)
 
         @pl.when(w > 0)
         def _():
             x_copy(chunk).start()
 
-        out_ref[0] = jnp.where(here, expand(last), out_ref[0])
+    def pack_chunk(chunk, carry):
+        for cell in range(2):
+            store_tiles(packed, pack(rhs, cell, chunk), cell, chunk)
+        return carry
+
+    def write_chunk(chunk, carry):
+        here = (iota((NC, LD), 1) >> line_bits) == chunk
+        out_ref[0] = jnp.where(here, expand(load_tiles(xc, chunk)), out_ref[0])
+        out_ref[1] = jnp.where(here, expand(load_tiles(upper_x, chunk)), out_ref[1])
+        return carry
 
     out_ref[...] = jnp.zeros((2, NC, LD), F32)
 
@@ -337,6 +355,10 @@
         is_forward = jnp.where(w == 3, t % 2 == 0, t < CH)
         chunk = jnp.where(w == 3, t // 2, t % CH)
 
+        first_pack = jnp.where(w == 0, chunk, jnp.where(t == 0, 0, CH))
+        last_pack = jnp.where(w == 0, jnp.where(is_forward, chunk + 1, chunk), CH)
+        lax.fori_loop(first_pack, last_pack, pack_chunk, 0)
+
         @pl.when(is_forward)
         def _():
             forward(chunk)
@@ -345,6 +367,9 @@
         def _():
             backward(chunk)
 
+        first_write = jnp.where(w == 3, jnp.where(t == 2 * CH - 1, 0, CH), chunk)
+        last_write = jnp.where(w == 3, CH, jnp.where(is_forward, chunk, chunk + 1))
+        lax.fori_loop(first_write, last_write, write_chunk, 0)
         return carry
 
     lax.fori_loop(0, 2 * CH, step, 0)
@@ -390,13 +415,16 @@
         pltpu.VMEM((8, NC, LD), F32),
         pltpu.VMEM((8, LD, 4 * LD), BF16),
         pltpu.VMEM((4, 2 * LD, 8 * LD), BF16),
-        pltpu.VMEM((4, 2 * NC, 8 * LD), BF16),
+        pltpu.VMEM((4, 8 * LD, 2 * LD), BF16),
+        pltpu.VMEM((2 * NC, 8 * LD), BF16),
         pltpu.VMEM((8, NC, LD), F32),
         pltpu.VMEM((2, 4, NC, LD), F32),
         pltpu.VMEM((2, NC, LD), F32),
+        pltpu.VMEM((2, CH, CR, LD), F32),
         pltpu.VMEM((CH, CR, LD), F32),
         pltpu.VMEM((CH, CR, LD), F32),
         pltpu.VMEM((2, CH, CR, LD), F32),
+        pltpu.VMEM((CH, CR, LD), F32),
         pltpu.VMEM((CH, CR, LD), F32),
         pltpu.VMEM((CH, CR, LD), F32),
         dma((6,)), dma((6,)),
@@ -410,7 +438,7 @@
         out_specs=pl.BlockSpec(memory_space=pltpu.VMEM),
         scratch_shapes=scratch,
         compiler_params=pltpu.CompilerParams(
-            collective_id=0, has_side_effects=True, vmem_limit_bytes=62 * 2**20
+            collective_id=0, has_side_effects=True, vmem_limit_bytes=63 * 2**20
         ),
         name="relax",
     )(*args)

time: 46 us -> 44.6 us (0.970)
  Pallas kernels: 43.6 us -> 42.3 us
    pallas_call x1, Pallas kernels: 43.6 us -> 42.3 us  [local(): pl.pallas_call(kernel, out_shape=jax.ShapeDtypeStruct((2, NC, LD), F32),...]
where the time goes in v2:
time: 44.6 us; the launch traced here: 44.5 us
  Pallas kernels  42.3 us (95%)
  local copies, waits for them, and re-layouts  1.55 us (3%)
  between operations  0.66 us (1%)
    pallas_call x1, Pallas kernels, local(): pl.pallas_call(kernel, out_shape=jax.ShapeDtypeStruct((2, NC, LD), F32),...  42.3 us
    unnamed x1, local copies, waits for them, and re-layouts  1.55 us

profile of v2, /device:TPU:0, one launch (start us, length us, event | category | flops | bytes accessed | tf_op | source)
XLA Modules:
  0.0 44.5 jit_solution(34599126259532184)
XLA Ops:
  0.7 42.3 %relax.1 = f32[2,112,128]{2,1,0:T(8,128)} custom-call(bf16[2,112,112,128]{3,2,1,0:T(8,128)(2,1)} %low_hbm.1, bf16[2,112,112,128]{3,2,1,0:T(8,128)(2,1)} %inv_hbm.1, bf16[2,112,112,128]{3,2,1,0:T(8,128)(2,1)} %upp_hbm.1, f32[2,112,128]{2,1,0:T(8,128)} %res_hbm.1, f32[2,112,128]{2,1,0:T(8,128)} %prev_hbm.1, s32[1,32,64]{2,1,0:T(8,128)} %sl_hbm.1, ...), custom_call_target="tpu_custom_call" | custom-call | tf_op jit(solution)/shard_map/relax/pallas_call | solution.py:434
  42.9 1.6 %copy.12 = f32[2,112,128]{2,1,0:T(8,128)} copy(f32[2,112,128]{2,1,0:T(8,128)} %relax.1) | data formatting | bytes 229376

commit v3 on v2

--- a/solution.py
+++ b/solution.py
@@ -106,6 +106,13 @@
 
     ring = [lambda v, d=d: lax.rem(v + d, 4) for d in (2, 1, 3)]
 
+    barrier = pltpu.get_barrier_semaphore()
+    partners = [dev(turn(x), z, core) for turn in ring for core in (0, 1)]
+    partners += [dev(x, turn(z), core) for turn in ring for core in (0, 1)]
+    partners += [dev(x, z, 1 - c), (lax.rem(w + 1, 4), span), (lax.rem(w + 3, 4), span)]
+    for partner in partners:
+        pl.semaphore_signal(barrier, inc=1, device_id=partner, device_id_type=MESH)
+
     smalls = [
         pltpu.make_async_copy(sl_hbm.at[0], sl, in_sem.at[0]),
         pltpu.make_async_copy(sc_hbm, sc, in_sem.at[1]),
@@ -121,15 +128,6 @@
     def stage_copy(m):
         return pltpu.make_async_copy(sources[m], stage.at[m % 3], stage_sem.at[m])
 
-    for m in range(3):
-        stage_copy(m).start()
-
-    barrier = pltpu.get_barrier_semaphore()
-    partners = [dev(turn(x), z, core) for turn in ring for core in (0, 1)]
-    partners += [dev(x, turn(z), core) for turn in ring for core in (0, 1)]
-    partners += [dev(x, z, 1 - c), (lax.rem(w + 1, 4), span), (lax.rem(w + 3, 4), span)]
-    for partner in partners:
-        pl.semaphore_signal(barrier, inc=1, device_id=partner, device_id_type=MESH)
 
     chunk_bits, line_bits = LD.bit_length() - 1, CL.bit_length() - 1
     n = iota((LD, 512), 1)
@@ -175,6 +173,9 @@
             src_ref=src, dst_ref=dst, send_sem=send_sem, recv_sem=recv_sem,
             device_id=device, device_id_type=MESH,
         )
+
+    for m in range(3):
+        stage_copy(m).start()
 
     pl.semaphore_wait(barrier, len(partners))
     started = []
@@ -333,6 +334,25 @@
         def _():
             x_copy(chunk).start()
 
+    def both(chunk):
+        y_copy(chunk).wait_recv()
+        done = chunk - 1
+        right = minus(load_tiles(yc, 1, done), load_tiles(edge, done))
+        lower = load_tiles(yc, 0, done)
+        ahead = load_tiles(packed, 0, chunk), load_tiles(packed, 1, chunk)
+        enter = matvec(mats.at[0, chunk], expand(load_tiles(yin, chunk)))
+        value = matvec(mats.at[3, done], expand(right))
+        first = minus(ahead[0], enter)
+        between = matvec(mats.at[1, chunk], expand(first))
+        back = matvec(mats.at[4, done], expand(value))
+        second = minus(ahead[1], between)
+        last = matvec(mats.at[5, done], expand(minus(lower, back)))
+        store_tiles(xc, last, done)
+        x_copy(done).start()
+        store_tiles(upper_x, value, done)
+        store_tiles(yc, first, 0, chunk)
+        store_tiles(yc, second, 1, chunk)
+
     def pack_chunk(chunk, carry):
         for cell in range(2):
             store_tiles(packed, pack(rhs, cell, chunk), cell, chunk)
@@ -347,13 +367,15 @@
     out_ref[...] = jnp.zeros((2, NC, LD), F32)
 
     def step(t, carry):
-        @pl.when(t == jnp.where(w == 3, 0, CH))
+        @pl.when(t == jnp.where(w >= 2, 0, CH))
         def _():
             for m in (3, 4, 5):
                 relayout(m)
 
-        is_forward = jnp.where(w == 3, t % 2 == 0, t < CH)
-        chunk = jnp.where(w == 3, t // 2, t % CH)
+        is_forward = t < jnp.where(w == 3, 1, CH)
+        is_both = (w == 3) & (t > 0) & (t < CH)
+        is_backward = (t >= CH) & (t < jnp.where(w == 3, CH + 1, 2 * CH))
+        chunk = jnp.where(w == 3, jnp.where(t == 0, 0, CH - 1), t % CH)
 
         first_pack = jnp.where(w == 0, chunk, jnp.where(t == 0, 0, CH))
         last_pack = jnp.where(w == 0, jnp.where(is_forward, chunk + 1, chunk), CH)
@@ -363,11 +385,15 @@
         def _():
             forward(chunk)
 
-        @pl.when(jnp.logical_not(is_forward))
+        @pl.when(is_both)
+        def _():
+            both(t)
+
+        @pl.when(is_backward)
         def _():
             backward(chunk)
 
-        first_write = jnp.where(w == 3, jnp.where(t == 2 * CH - 1, 0, CH), chunk)
+        first_write = jnp.where(w == 3, jnp.where(t == CH, 0, CH), chunk)
         last_write = jnp.where(w == 3, CH, jnp.where(is_forward, chunk, chunk + 1))
         lax.fori_loop(first_write, last_write, write_chunk, 0)
         return carry

time: 44.6 us -> 44.5 us (level)
  no operation moved by 1% of the time
where the time goes in v3:
time: 44.5 us; the launch traced here: 44.3 us
  Pallas kernels  42.1 us (95%)
  local copies, waits for them, and re-layouts  1.55 us (3%)
  between operations  0.66 us (1%)
    pallas_call x1, Pallas kernels, local(): pl.pallas_call(kernel, out_shape=jax.ShapeDtypeStruct((2, NC, LD), F32),...  42.1 us
    unnamed x1, local copies, waits for them, and re-layouts  1.55 us

profile of v3, /device:TPU:0, one launch (start us, length us, event | category | flops | bytes accessed | tf_op | source)
XLA Modules:
  0.0 44.3 jit_solution(10461382859598318391)
XLA Ops:
  0.7 42.1 %relax.1 = f32[2,112,128]{2,1,0:T(8,128)} custom-call(bf16[2,112,112,128]{3,2,1,0:T(8,128)(2,1)} %low_hbm.1, bf16[2,112,112,128]{3,2,1,0:T(8,128)(2,1)} %inv_hbm.1, bf16[2,112,112,128]{3,2,1,0:T(8,128)(2,1)} %upp_hbm.1, f32[2,112,128]{2,1,0:T(8,128)} %res_hbm.1, f32[2,112,128]{2,1,0:T(8,128)} %prev_hbm.1, s32[1,32,64]{2,1,0:T(8,128)} %sl_hbm.1, ...), custom_call_target="tpu_custom_call" | custom-call | tf_op jit(solution)/shard_map/relax/pallas_call | solution.py:460
  42.8 1.6 %copy.12 = f32[2,112,128]{2,1,0:T(8,128)} copy(f32[2,112,128]{2,1,0:T(8,128)} %relax.1) | data formatting | bytes 229376
